TPU v7x, 32 devices: a whole 2x2x4 slice. The times are simulated.
32 devices in a mesh: val: 4 (over y, core), cond: 8 (over z, x).
Axes of the slice: x: 2, y: 2, z: 4, core: 2. Of those that a mesh axis runs over, the one named last changes fastest.
Arguments:
- orb_val: bfloat16 [2, 4, 262144], P(None, 'val'), may hold values from -6 to 6
- orb_cond: bfloat16 [2, 8, 262144], P(None, 'cond'), may hold values from -6 to 6
- energies: float32 [4, 8], replicated, may hold values from 0.2 to 2
- gvec_map: int32 [8192], replicated, may hold values from 0 to 262143, as said below
Outputs:
- chi_zero: float32 [2, 8192, 8192], P(None, 'val', 'cond')
Inputs may be any that keep to these rules, and one draw needn't show every extreme that they name: `gvec_map`: the 8192 entries are distinct grid cells, the 8192 cells nearest the anchor in signed frequencies (each index k read as k - 64 when k >= 32), ties on the sphere's surface broken at random, listed in random order; at the real sizes they lie within a sphere of radius about 12.5 grid units.
All inputs are finite; a program needn't handle non-finite values.
Results may differ from a plain program's by a relative error of at most 0.0048.
Values may be sent and summed in bfloat16 or wider, within the bound.
A program may use at most 64 MiB of HBM per device.

v0:
```python
import math

import jax
import jax.numpy as jnp
import numpy as np
from jax import lax
from jax.sharding import PartitionSpec as P

NFFT = 64
NG = 8192


def kept_waves(side, count_g):
    wave = np.arange(side)
    signed = np.where(wave >= side // 2, wave - side, wave)
    squares = signed * signed
    radius = (squares[:, None, None] + squares[None, :, None] + squares[None, None, :]).reshape(-1)
    limit = int(np.sort(radius)[count_g - 1])
    reach = math.isqrt(limit)
    kept = [int(k) for k in wave if abs(int(signed[k])) <= reach]
    position = np.zeros(side, dtype=np.int32)
    for order_pos, wave_idx in enumerate(kept):
        position[wave_idx] = order_pos
    return (np.array(kept, dtype=np.int32), position)


def dft_rows(kept, side):
    grid_pts = np.arange(side, dtype=np.int64)
    phase = kept.astype(np.int64)[:, None] * grid_pts[None, :] % side
    angle_grid = jnp.asarray(phase.astype(np.int32)).astype(jnp.float32) * (2.0 * math.pi / side)
    return (jnp.cos(angle_grid), jnp.sin(angle_grid))


def section(real_plane, imag_plane, cosine, sine, pattern):
    highest = lax.Precision.HIGHEST
    new_real = jnp.einsum(pattern, real_plane, cosine, precision=highest) + jnp.einsum(
        pattern, imag_plane, sine, precision=highest
    )
    new_imag = jnp.einsum(pattern, imag_plane, cosine, precision=highest) - jnp.einsum(
        pattern, real_plane, sine, precision=highest
    )
    return (new_real, new_imag)


def on_device(orb_val, orb_cond, energies, gvec_map):
    side = NFFT
    count = orb_cond.shape[1]
    total_val = energies.shape[0]
    total_cond = energies.shape[1]
    val_pos = lax.axis_index("val")
    cond_pos = lax.axis_index("cond")
    kept, position = kept_waves(side, NG)
    width = int(kept.shape[0])
    cosine, sine = dft_rows(kept, side)
    val_real = orb_val[0].astype(jnp.float32)
    val_imag = orb_val[1].astype(jnp.float32)
    cond_real = orb_cond[0].astype(jnp.float32)
    cond_imag = orb_cond[1].astype(jnp.float32)
    pair_real = (val_real * cond_real + val_imag * cond_imag).reshape(count, side, side, side)
    pair_imag = (val_real * cond_imag - val_imag * cond_real).reshape(count, side, side, side)
    pair_real, pair_imag = section(pair_real, pair_imag, cosine, sine, "bxyn,kn->bxyk")
    pair_real, pair_imag = section(pair_real, pair_imag, cosine, sine, "bxnz,kn->bxkz")
    pair_real, pair_imag = section(pair_real, pair_imag, cosine, sine, "bnyz,kn->bkyz")
    scale = float(side) ** (-1.5)
    cube_real = pair_real.reshape(count, -1) * scale
    cube_imag = pair_imag.reshape(count, -1) * scale
    lookup = jnp.asarray(position)
    plane = jnp.take(lookup, gvec_map // (side * side))
    line = jnp.take(lookup, gvec_map // side % side)
    column = jnp.take(lookup, gvec_map % side)
    cube_index = (plane * width + line) * width + column
    real_part = jnp.take(cube_real, cube_index, axis=1)
    imag_part = jnp.take(cube_imag, cube_index, axis=1)
    density = jnp.stack([real_part, imag_part])[:, None].astype(jnp.bfloat16)
    weight_all = -2.0 / (float(total_val * total_cond) * energies)
    weight_local = lax.dynamic_slice(weight_all, (val_pos, cond_pos * count), (1, count))
    weighted = (weight_local[None, :, :, None] * density.astype(jnp.float32)).astype(jnp.bfloat16)
    rows = lax.all_to_all(weighted, "val", split_axis=3, concat_axis=1, tiled=True)
    col_part = lax.all_to_all(density, "cond", split_axis=3, concat_axis=2, tiled=True)
    cols = lax.all_gather(col_part, "val", axis=1, tiled=True)
    rows_all = lax.all_gather(rows, "cond", axis=2, tiled=True)
    left = rows_all.reshape(-1, rows_all.shape[3])
    right = cols.reshape(-1, cols.shape[3])
    turned = jnp.concatenate([-cols[1:2], cols[0:1]], axis=0).reshape(-1, cols.shape[3])
    dims = (((0,), (0,)), ((), ()))
    real_sum = lax.dot_general(left, right, dims, preferred_element_type=jnp.float32)
    imag_sum = lax.dot_general(left, turned, dims, preferred_element_type=jnp.float32)
    return jnp.stack([real_sum, imag_sum])


def solution(mesh):
    return jax.shard_map(
        on_device,
        mesh=mesh,
        in_specs=(P(None, "val", None), P(None, "cond", None), P(), P()),
        out_specs=P(None, "val", "cond"),
        check_vma=False,
    )
```

profile of v0, /device:TPU:0, one launch (start us, length us, event | category | flops | bytes accessed | tf_op | source)
XLA Modules:
  0.0 351.5 jit_solution(5092542832205861981)
XLA Ops:
  0.0 0.7 multiply_divide_fusion
  0.7 1.3 broadcast_clamp_fusion
  2.0 14.1 %add_reduce_fusion = (f32[262144]{0:T(1024)}, f32[262144]{0:T(1024)S(1)}) fusion(bf16[2,1,262144]{2,0,1:T(2,128)(2,1)} %param.11, bf16[2,1,262144]{2,0,1:T(2,128)(2,1)} %param.10), kind=kLoop, calls=%fused_computation.16 | loop fusion | flops 2621440 | bytes 4194304 | tf_op jit(solution)/shard_map/add | solution.py:59
  16.1 2.1 add.67
  18.2 0.0 copy-start.2
  18.2 1.7 sub.39
  19.8 5.8 %fusion.28 = f32[64,64,25]{1,2,0:T(8,128)S(1)} fusion(f32[64,64,64]{2,1,0:T(8,128)S(1)} %add.67, f32[25,64,1]{1,0,2:T(8,128)S(1)} %copy-done.2), kind=kOutput, calls=%fused_computation.72 | convolution fusion | flops 78643200 | bytes 1464576 | tf_op jit(solution)/shard_map/bxyn,kn->bxyk/dot_general | solution.py:36
  25.6 0.0 copy-start.1
  25.6 5.8 %fusion.29 = f32[64,64,25]{1,2,0:T(8,128)S(1)} fusion(f32[64,64,64]{2,1,0:T(8,128)S(1)} %copy-done, f32[25,64,1]{1,0,2:T(8,128)S(1)} %copy-done.2), kind=kOutput, calls=%fused_computation.73 | convolution fusion | flops 78643200 | bytes 1464576 | tf_op jit(solution)/shard_map/bxyn,kn->bxyk/dot_general | solution.py:39
  31.4 5.8 %convolution_add_fusion = f32[64,64,25]{1,2,0:T(8,128)S(1)} fusion(f32[64,64,25]{1,2,0:T(8,128)S(1)} %fusion.28, f32[64,64,64]{2,1,0:T(8,128)S(1)} %copy-done, f32[25,64,1]{1,0,2:T(8,128)S(1)} %copy-done.1), kind=kOutput, calls=%fused_computation.6 | convolution fusion | flops 78745600 | bytes 1874176 | tf_op jit(solution)/shard_map/bxyn,kn->bxyk/dot_general | solution.py:36
  37.2 5.9 %convolution_subtract_fusion = f32[64,64,25]{1,2,0:T(8,128)S(1)} fusion(f32[64,64,25]{1,2,0:T(8,128)S(1)} %fusion.29, f32[64,64,64]{2,1,0:T(8,128)S(1)} %add.67, f32[25,64,1]{1,0,2:T(8,128)S(1)} %copy-done.1), kind=kOutput, calls=%fused_computation.5 | convolution fusion | flops 78745600 | bytes 1874176 | tf_op jit(solution)/shard_map/bxyn,kn->bxyk/dot_general | solution.py:39
  43.1 2.3 fusion.4
  45.5 2.3 fusion.8
  47.8 2.3 fusion.2
  50.1 2.3 fusion.3
  52.4 1.8 fusion.14
  54.2 1.8 fusion.10
  56.0 1.8 fusion
  57.8 2.0 fusion.1
  59.8 0.2 copy.82
  60.0 0.2 reshape.435
  60.2 0.2 copy.79
  60.4 0.2 reshape.432
  60.7 45.5 %gather_fusion.1 = f32[8192]{0:T(1024)S(1)} fusion(f32[15625]{0:T(1024)S(1)} %reshape.435, s32[8192]{0:T(1024)S(1)} %get-tuple-element.13), kind=kCustom, calls=%fused_computation.1.clone | custom fusion | bytes 98304 | tf_op jit(solution)/shard_map/jit(_take)/gather | solution.py:73
  106.2 45.5 %gather_fusion = f32[8192]{0:T(1024)S(1)} fusion(f32[15625]{0:T(1024)S(1)} %reshape.432, s32[8192]{0:T(1024)S(1)} %get-tuple-element.13), kind=kCustom, calls=%fused_computation.clone | custom fusion | bytes 98304 | tf_op jit(solution)/shard_map/jit(_take)/gather | solution.py:72
  151.8 0.1 pad_maximum_fusion.1
  151.9 0.6 dynamic_slice.3
  152.5 0.7 multiply_convert_fusion
  153.3 6.8 %copy.83 = bf16[2,1,1,8192]{0,2,1,3:T(2,128)(2,1)} copy(bf16[2,1,1,8192]{3,0,2,1:T(2,128)(2,1)S(1)} %get-tuple-element.9) | data formatting | bytes 65536 | tf_op jit(solution)/shard_map/convert_element_type | solution.py:77
  160.0 0.5 broadcast.774
  160.6 45.2 %reduce.8 = bf16[8192,2]{1,0:T(8,128)(2,1)S(1)} reduce(bf16[8192,1,1,2]{3,2,1,0:T(2,128)(2,1)} %bitcast.66, bf16[]{:T(256)} %broadcast.774), dimensions={1,2}, to_apply=%bitcast.44.reduce_sub_computation | reduce | bytes 65538
  205.7 3.8 %reshape.456 = bf16[4,2,2048]{2,1,0:T(2,128)(2,1)} reshape(bf16[8192,2]{1,0:T(8,128)(2,1)S(1)} %reduce.8) | data formatting | bytes 65536
  209.6 4.5 %all-to-all-start = ((bf16[4,2,2048]{2,1,0:T(2,128)(2,1)}), bf16[4,2,2048]{2,1,0:T(2,128)(2,1)S(1)}, u32[]{:S(2)}, u32[]{:S(2)}) async-start(bf16[4,2,2048]{2,1,0:T(2,128)(2,1)} %reshape.456), calls=%async_computation | async-start | bytes 65536 | tf_op jit(solution)/shard_map/all_to_all | solution.py:78
  214.1 6.8 %copy.85 = bf16[2,1,1,8192]{0,2,1,3:T(2,128)(2,1)} copy(bf16[2,1,1,8192]{3,0,2,1:T(2,128)(2,1)S(1)} %get-tuple-element.10) | data formatting | bytes 65536 | tf_op jit(solution)/shard_map/convert_element_type | solution.py:74
  220.8 45.2 %reduce.9 = bf16[8192,2]{1,0:T(8,128)(2,1)S(1)} reduce(bf16[8192,1,1,2]{3,2,1,0:T(2,128)(2,1)} %bitcast.67, bf16[]{:T(256)} %broadcast.774), dimensions={1,2}, to_apply=%bitcast.46.reduce_sub_computation | reduce | bytes 65538
  266.0 3.8 %reshape.458 = bf16[8,2,1024]{2,1,0:T(2,128)(2,1)} reshape(bf16[8192,2]{1,0:T(8,128)(2,1)S(1)} %reduce.9) | data formatting | bytes 65536
  269.8 6.3 %all-to-all-start.1 = ((bf16[8,2,1024]{2,1,0:T(2,128)(2,1)}), bf16[8,2,1024]{2,1,0:T(2,128)(2,1)S(1)}, u32[]{:S(2)}, u32[]{:S(2)}) async-start(bf16[8,2,1024]{2,1,0:T(2,128)(2,1)} %reshape.458), calls=%async_computation.1 | async-start | bytes 65536 | tf_op jit(solution)/shard_map/all_to_all | solution.py:79
  276.1 5.9 %reshape.457 = bf16[8192,1,1,2]{3,2,1,0:T(2,128)(2,1)} reshape(bf16[4,2,2048]{2,1,0:T(2,128)(2,1)S(1)} %all-to-all-done) | data formatting | bytes 65536
  282.1 8.1 %copy.84 = bf16[2,1,1,8192]{3,0,2,1:T(2,128)(2,1)S(1)} copy(bf16[2,1,1,8192]{0,2,1,3:T(2,128)(2,1)} %bitcast.68) | data formatting | bytes 65536 | tf_op jit(solution)/shard_map/all_to_all | solution.py:78
  290.2 31.3 %all_gather.6 = bf16[2,4,8,2048]{3,1,0,2:T(4,128)(2,1)S(1)} all-gather(bf16[2,4,1,2048]{3,1,0,2:T(4,128)(2,1)S(1)} %all_to_all.9), channel_id=1, replica_groups=mesh['val'=4,'cond'=8] {'cond'}, dimensions={2}, use_global_device_ids=true | all-gather | bytes 294912 | tf_op jit(solution)/shard_map/all_gather | solution.py:81
  321.5 6.2 %reshape.459 = bf16[8192,1,1,2]{3,2,1,0:T(2,128)(2,1)} reshape(bf16[8,2,1024]{2,1,0:T(2,128)(2,1)S(1)} %all-to-all-done.1) | data formatting | bytes 65536
  327.7 8.1 %copy.86 = bf16[2,1,1,8192]{3,0,2,1:T(2,128)(2,1)S(1)} copy(bf16[2,1,1,8192]{0,2,1,3:T(2,128)(2,1)} %bitcast.69) | data formatting | bytes 65536 | tf_op jit(solution)/shard_map/all_to_all | solution.py:79
  335.8 6.0 %all_gather.7 = bf16[2,4,8,1024]{3,2,0,1:T(8,128)(2,1)S(1)} all-gather(bf16[2,1,8,1024]{3,2,0,1:T(8,128)(2,1)S(1)} %bitcast.71), channel_id=1, replica_groups=mesh['val'=4,'cond'=8] {'val'}, dimensions={1}, use_global_device_ids=true | all-gather | bytes 163840 | tf_op jit(solution)/shard_map/all_gather | solution.py:80
  341.8 0.1 copy.88
  341.9 0.1 slice_negate_fusion
  342.0 1.4 convolution_bitcast_fusion.1
  343.4 1.4 convolution_bitcast_fusion
  344.8 6.2 %pad_maximum_fusion = f32[2,2048,1024]{2,1,0:T(8,128)} fusion(f32[1,2048,1024]{2,1,0:T(8,128)S(1)} %convolution_bitcast_fusion, f32[1,2048,1024]{2,1,0:T(8,128)S(1)} %convolution_bitcast_fusion.1), kind=kLoop, calls=%fused_computation.2 | loop fusion | flops 4194304 | bytes 33554432 | tf_op jit(solution)/shard_map/stack | solution.py:88
  (11 shorter events, 0.1 us)
Async XLA Ops:
  18.2 1.7 copy-start.2
  19.8 5.8 %copy-start = (f32[64,64,64]{2,1,0:T(8,128)S(1)}, f32[64,64,64]{2,1,0:T(8,128)}, u32[]{:S(2)}) copy-start(f32[64,64,64]{2,1,0:T(8,128)} %sub.39) | copy-start | bytes 3145732
  25.6 5.8 %copy-start.1 = (f32[25,64,1]{1,0,2:T(8,128)S(1)}, f32[25,64,1]{1,0,2:T(8,128)}, u32[]{:S(2)}) copy-start(f32[25,64,1]{1,0,2:T(8,128)} %constant.868) | copy-start | bytes 19204
  209.6 60.3 %all-to-all-start = ((bf16[4,2,2048]{2,1,0:T(2,128)(2,1)}), bf16[4,2,2048]{2,1,0:T(2,128)(2,1)S(1)}, u32[]{:S(2)}, u32[]{:S(2)}) async-start(bf16[4,2,2048]{2,1,0:T(2,128)(2,1)} %reshape.456), calls=%async_computation | async-start | bytes 65536 | tf_op jit(solution)/shard_map/all_to_all | solution.py:78
  269.8 51.6 %all-to-all-start.1 = ((bf16[8,2,1024]{2,1,0:T(2,128)(2,1)}), bf16[8,2,1024]{2,1,0:T(2,128)(2,1)S(1)}, u32[]{:S(2)}, u32[]{:S(2)}) async-start(bf16[8,2,1024]{2,1,0:T(2,128)(2,1)} %reshape.458), calls=%async_computation.1 | async-start | bytes 65536 | tf_op jit(solution)/shard_map/all_to_all | solution.py:79
where the time goes:
time: 357 us; the launch traced here: 352 us
  local copies, waits for them, and re-layouts  146 us (41%)
  other arithmetic  114 us (32%)
  matrix products  42.7 us (12%)
  blocking collectives  37.3 us (10%)
  starting transfers between devices  10.8 us (3%)
    unnamed x2, other arithmetic  90.4 us
    gather x1, local copies, waits for them, and re-layouts, on_device(): imag_part = jnp.take(cube_imag, cube_index, axis=1)  45.5 us
    gather x1, local copies, waits for them, and re-layouts, on_device(): real_part = jnp.take(cube_real, cube_index, axis=1)  45.5 us
    all_gather x1, blocking collectives, on_device(): rows_all = lax.all_gather(rows, 'cond', axis=2, tiled=True)  31.3 us
    unnamed x12, local copies, waits for them, and re-layouts  20.4 us
    add x1, other arithmetic, on_device(): val_real * cond_real + val_imag * cond_imag  14.1 us
    dot_general x3, matrix products, section(): jnp.einsum(pattern, real_plane, sine, precision=highest)  10.2 us
    dot_general x3, matrix products, section(): jnp.einsum(pattern, imag_plane, sine, precision=highest)  9.89 us
  transfers between devices with their start and end apart: 2, of which 0 were waited for; matrix products, arithmetic and copies ran while one was open for 20% of the time, Pallas kernels for 0%

commit v1 on v0

v1 whole, which is shorter than its diff:
```python
import functools
import math

import jax
import jax.numpy as jnp
import ml_dtypes
import numpy as np
from jax import lax
from jax.experimental import pallas as pl
from jax.experimental.pallas import tpu as pltpu
from jax.sharding import PartitionSpec as P

SIDE = 64
PAD = 32
F32 = jnp.float32
BF16 = jnp.bfloat16


def reach_of(side, count_g):
    wave = np.arange(side)
    signed = np.where(wave >= side // 2, wave - side, wave)
    squares = signed * signed
    radius = (squares[:, None, None] + squares[None, :, None] + squares[None, None, :]).reshape(-1)
    return math.isqrt(int(np.sort(radius)[count_g - 1]))


def split_high_low(matrix, axis):
    high = matrix.astype(ml_dtypes.bfloat16)
    low = (matrix - high.astype(np.float64)).astype(ml_dtypes.bfloat16)
    return np.concatenate([high, high, low], axis=axis)


def dft_matrices(reach):
    width = 2 * reach + 1
    waves = np.arange(width) - reach
    angle = 2.0 * np.pi * ((waves[None, :] * np.arange(SIDE)[:, None]) % SIDE) / SIDE
    cosine = np.zeros((SIDE, PAD))
    sine = np.zeros((SIDE, PAD))
    cosine[:, :width] = np.cos(angle)
    sine[:, :width] = np.sin(angle)
    full = np.zeros((2, SIDE, 2, PAD))
    full[0, :, 0] = cosine
    full[1, :, 0] = sine
    full[0, :, 1] = -sine
    full[1, :, 1] = cosine
    along_z = np.zeros((2, 2, SIDE, 2, 2, PAD))
    for low in range(2):
        along_z[:, low, :, :, low, :] = full
    along_z = along_z.reshape(4 * SIDE, 4 * PAD)
    along_y = full.reshape(2, SIDE // 2, 2, 2, PAD).transpose(3, 4, 0, 2, 1).reshape(2 * PAD, 2 * SIDE)
    along_x = full.transpose(2, 3, 0, 1).reshape(2 * PAD, 2 * SIDE) * float(SIDE) ** -1.5
    return split_high_low(along_z, 0), split_high_low(along_y, 1), split_high_low(along_x, 1)


def high_low(value):
    high = value.astype(BF16)
    return high, (value - high.astype(F32)).astype(BF16)


def regroup(parts, lane):
    results = []
    for j in range(4):
        total = None
        for i, part in enumerate(parts):
            shift = (32 * (i - j)) % 128
            moved = pltpu.roll(part, shift, 1) if shift else part
            total = moved if total is None else jnp.where(lane == i, moved, total)
        results.append(total)
    return results


def cube_of(val_ref, cond_ref, along_z, along_y, along_x, val_wide, cond_wide, by_z, by_y, quads):
    half = SIDE // 2
    val_wide[...] = val_ref[...].astype(F32)
    cond_wide[...] = cond_ref[...].astype(F32)
    quarter = SIDE // 4
    for x_high in range(quarter):
        rows = 4 * half
        real_rows = pl.ds(2 * rows * x_high, rows, stride=2)
        imag_rows = pl.ds(2 * rows * x_high + 1, rows, stride=2)
        val_real, val_imag = val_wide[real_rows, :], val_wide[imag_rows, :]
        cond_real, cond_imag = cond_wide[real_rows, :], cond_wide[imag_rows, :]
        real_high, real_low = high_low(val_real * cond_real + val_imag * cond_imag)
        imag_high, imag_low = high_low(val_real * cond_imag - val_imag * cond_real)
        for x_low in range(4):
            here = slice(half * x_low, half * (x_low + 1))
            there = slice(half * x_high, half * (x_high + 1))
            pieces = (real_high, imag_high, real_low, imag_low, real_high, imag_high)
            for at, piece in enumerate(pieces):
                by_z[x_low, there, 128 * at : 128 * (at + 1)] = piece[here]
    lane = lax.broadcasted_iota(jnp.int32, (1, 128), 1) // 32
    step = 128
    for start in range(0, quarter * half, step):
        parts = [
            jnp.dot(by_z[x_low, start : start + step, :], along_z[...], preferred_element_type=F32)
            for x_low in range(4)
        ]
        grouped = regroup(parts, lane)
        for inner in range(step // half):
            block = jnp.concatenate([g[half * inner : half * (inner + 1)] for g in grouped], axis=0)
            high, low = high_low(block)
            stacked = jnp.concatenate([high, low, high], axis=0)
            turned = jnp.dot(along_y[...], stacked, preferred_element_type=F32)
            x_high = start // half + inner
            by_y[128 * x_high : 128 * (x_high + 1), :] = jnp.concatenate([turned, turned], axis=0).T
    cubes = []
    for quad in range(quads):
        blocks = [by_y[pl.ds(4 * quad + i, SIDE, stride=PAD), :] for i in range(4)]
        real, imag = regroup(blocks, lane)[:2]
        high, low = high_low(jnp.concatenate([real, imag], axis=0))
        stacked = jnp.concatenate([high, low, high], axis=0)
        cubes.append(jnp.dot(along_x[...], stacked, preferred_element_type=F32).astype(BF16))
    return jnp.concatenate(cubes, axis=1)


def pick(cube, cells, reach):
    count = cells.shape[1]
    x_pos = ((cells >> 12) + reach) & (SIDE - 1)
    y_pos = ((cells >> 6) + reach) & (SIDE - 1)
    z_pos = (cells + reach) & (SIDE - 1)
    place = z_pos * PAD + y_pos
    rows = lax.broadcasted_iota(jnp.int32, (cube.shape[1], count), 0)
    chosen = jnp.where(rows == place, 1.0, 0.0).astype(BF16)
    lines = jnp.dot(cube, chosen, preferred_element_type=F32)
    plane = lax.broadcasted_iota(jnp.int32, (PAD, count), 0) == x_pos
    real = jnp.sum(jnp.where(plane, lines[:PAD], 0.0), axis=0, keepdims=True)
    imag = jnp.sum(jnp.where(plane, lines[PAD:], 0.0), axis=0, keepdims=True)
    return real, imag


def density_kernel(reach, val_ref, cond_ref, gvec_ref, wz_ref, wy_ref, wx_ref, out_ref, *scratch):
    quads = (2 * reach + 1 + 3) // 4
    cube_ref = scratch[-1]
    cube_ref[...] = cube_of(val_ref, cond_ref, wz_ref, wy_ref, wx_ref, *scratch[:-1], quads)
    step = 512

    @pl.loop(0, out_ref.shape[1] // step)
    def _(at):
        here = pl.ds(pl.multiple_of(at * step, step), step)
        real, imag = pick(cube_ref[...], gvec_ref[:, here], reach)
        out_ref[0:1, here] = real
        out_ref[1:2, here] = imag


def flat_rows(orbital):
    return orbital.reshape(2, -1, 128).transpose(1, 0, 2).reshape(-1, 128)


def on_device(orb_val, orb_cond, energies, gvec_map):
    count_g = gvec_map.shape[0]
    reach = reach_of(SIDE, count_g)
    along_z, along_y, along_x = dft_matrices(reach)
    rows = 2 * SIDE**3 // 128
    quads = (2 * reach + 1 + 3) // 4
    dense = pl.pallas_call(
        functools.partial(density_kernel, reach),
        out_shape=jax.ShapeDtypeStruct((2, count_g), F32),
        in_specs=[pl.BlockSpec(memory_space=pltpu.VMEM)] * 6,
        out_specs=pl.BlockSpec(memory_space=pltpu.VMEM),
        scratch_shapes=[
            pltpu.VMEM((rows, 128), F32),
            pltpu.VMEM((rows, 128), F32),
            pltpu.VMEM((4, SIDE // 4 * SIDE // 2, 6 * 128), BF16),
            pltpu.VMEM((SIDE * PAD, 128), F32),
            pltpu.VMEM((2 * PAD, 128 * quads), BF16),
        ],
        compiler_params=pltpu.CompilerParams(vmem_limit_bytes=48 * 2**20),
        name="density",
    )(
        flat_rows(orb_val),
        flat_rows(orb_cond),
        gvec_map.reshape(1, count_g),
        jnp.asarray(along_z),
        jnp.asarray(along_y),
        jnp.asarray(along_x),
    )
    total_val, total_cond = energies.shape
    val_pos = lax.axis_index("val")
    cond_pos = lax.axis_index("cond")
    density = dense[:, None, None, :].astype(BF16)
    weight_all = -2.0 / (float(total_val * total_cond) * energies)
    weight_local = lax.dynamic_slice(weight_all, (val_pos, cond_pos), (1, 1))
    weighted = (weight_local[None, :, :, None] * density.astype(F32)).astype(BF16)
    rows = lax.all_to_all(weighted, "val", split_axis=3, concat_axis=1, tiled=True)
    col_part = lax.all_to_all(density, "cond", split_axis=3, concat_axis=2, tiled=True)
    cols = lax.all_gather(col_part, "val", axis=1, tiled=True)
    rows_all = lax.all_gather(rows, "cond", axis=2, tiled=True)
    left = rows_all.reshape(-1, rows_all.shape[3])
    right = cols.reshape(-1, cols.shape[3])
    turned = jnp.concatenate([-cols[1:2], cols[0:1]], axis=0).reshape(-1, cols.shape[3])
    dims = (((0,), (0,)), ((), ()))
    real_sum = lax.dot_general(left, right, dims, preferred_element_type=F32)
    imag_sum = lax.dot_general(left, turned, dims, preferred_element_type=F32)
    return jnp.stack([real_sum, imag_sum])


def solution(mesh):
    return jax.shard_map(
        on_device,
        mesh=mesh,
        in_specs=(P(None, "val", None), P(None, "cond", None), P(), P()),
        out_specs=P(None, "val", "cond"),
        check_vma=False,
    )
```

time: 357 us -> 214 us (0.60); the launches traced: 352 us -> 213 us
  local copies, waits for them, and re-layouts: 146 us -> 56.5 us
  matrix products: 42.7 us -> 2.82 us
  other arithmetic: 114 us -> 98.2 us
  Pallas kernels: 0 us -> 7.77 us
    gather x2 -> x0, local copies, waits for them, and re-layouts: 91.1 us -> none  [the longest x1 45.5 us: on_device(): imag_part = jnp.take(cube_imag, cube_index, axis=1)]
    dot_general x14 -> x2, matrix products: 42.7 us -> 2.82 us  [the longest x1 1.41 us: on_device(): real_sum = lax.dot_general(left, right, dims, preferred_element_type=F32)]
    add x1 -> x0, other arithmetic: 14.1 us -> none  [on_device(): val_real * cond_real + val_imag * cond_imag]
    pallas_call x0 -> x1, Pallas kernels: none -> 7.77 us  [on_device(): pl.pallas_call(functools.partial(density_kernel, reach), out_shape=jax.Sh...]
    unnamed x12 -> x18, local copies, waits for them, and re-layouts: 20.4 us -> 26.1 us
  transfers between devices with their start and end apart: 2 -> 2, of which waited for: 0 -> 0; matrix products, arithmetic and copies ran while one was open for 20% -> 33% of each run, Pallas kernels for 0% -> 0%
where the time goes in v1:
time: 214 us; the launch traced here: 213 us
  other arithmetic  98.2 us (46%)
  local copies, waits for them, and re-layouts  56.5 us (26%)
  blocking collectives  37 us (17%)
  starting transfers between devices  10.8 us (5%)
  Pallas kernels  7.77 us (4%)
  matrix products  2.82 us (1%)
    unnamed x2, other arithmetic  90.5 us
    all_gather x1, blocking collectives, on_device(): rows_all = lax.all_gather(rows, 'cond', axis=2, tiled=True)  31.4 us
    unnamed x18, local copies, waits for them, and re-layouts  26.1 us
    all_to_all x2, local copies, waits for them, and re-layouts, on_device(): lax.all_to_all(weighted, 'val', split_axis=3, concat_axis=1, tiled=True)  8.1 us
    all_to_all x1, local copies, waits for them, and re-layouts, on_device(): lax.all_to_all(density, 'cond', split_axis=3, concat_axis=2, tiled=True)  8.07 us
    pallas_call x1, Pallas kernels, on_device(): pl.pallas_call(functools.partial(density_kernel, reach), out_shape=jax.Sh...  7.77 us
    convert_element_type x1, local copies, waits for them, and re-layouts, on_device(): (weight_local[None, :, :, None] * density.astype(F32)).astype(BF16)  6.76 us
    convert_element_type x1, local copies, waits for them, and re-layouts, on_device(): density = dense[:, None, None, :].astype(BF16)  6.71 us
  transfers between devices with their start and end apart: 2, of which 0 were waited for; matrix products, arithmetic and copies ran while one was open for 33% of the time, Pallas kernels for 0%

profile of v1, /device:TPU:0, one launch (start us, length us, event | category | flops | bytes accessed | tf_op | source)
XLA Modules:
  0.0 213.1 jit_solution(3532579463048676008)
XLA Ops:
  0.0 0.7 multiply_divide_fusion
  0.7 0.6 dynamic_slice.3
  1.3 0.0 copy-start
  1.3 1.2 copy-done
  2.5 0.0 copy-start.1
  2.5 1.2 copy-done.1
  3.7 0.0 copy-start.2
  3.7 0.9 copy-done.2
  4.7 0.0 copy-start.3
  4.7 0.8 copy-done.3
  5.5 0.0 copy-start.4
  5.5 0.8 copy-done.4
  6.3 0.0 copy-start.5
  6.3 0.8 copy-done.5
  7.0 7.8 %density.1 = f32[2,8192]{1,0:T(2,128)S(1)} custom-call(bf16[4096,128]{1,0:T(8,128)(2,1)S(1)} %bitcast.42, bf16[4096,128]{1,0:T(8,128)(2,1)S(1)} %bitcast.43, s32[1,8192]{1,0:T(1,128)S(1)} %bitcast.44, bf16[768,128]{1,0:T(8,128)(2,1)S(1)} %copy-done.2, bf16[64,384]{1,0:T(8,128)(2,1)S(1)} %copy-done.4, bf16[64,384]{1,0:T(8,128)(2,1)S(1)} %copy-done.3), custom_call_target="tpu_custom_call" | custom-call | tf_op jit(solution)/shard_map/density/pallas_call | solution.py:155
  14.8 0.7 convert_bitcast_fusion
  15.5 6.8 %copy.39 = bf16[2,1,1,8192]{0,2,1,3:T(2,128)(2,1)} copy(bf16[2,1,1,8192]{3,0,2,1:T(2,128)(2,1)S(1)} %get-tuple-element.8) | data formatting | bytes 65536 | tf_op jit(solution)/shard_map/convert_element_type | solution.py:183
  22.2 0.6 broadcast.2
  22.8 45.2 %reduce = bf16[8192,2]{1,0:T(8,128)(2,1)S(1)} reduce(bf16[8192,1,1,2]{3,2,1,0:T(2,128)(2,1)} %bitcast.45, bf16[]{:T(256)} %broadcast.2), dimensions={1,2}, to_apply=%bitcast.37.reduce_sub_computation | reduce | bytes 65538
  68.1 3.8 %reshape.38 = bf16[4,2,2048]{2,1,0:T(2,128)(2,1)} reshape(bf16[8192,2]{1,0:T(8,128)(2,1)S(1)} %reduce) | data formatting | bytes 65536
  71.9 4.2 %all-to-all-start = ((bf16[4,2,2048]{2,1,0:T(2,128)(2,1)}), bf16[4,2,2048]{2,1,0:T(2,128)(2,1)S(1)}, u32[]{:S(2)}, u32[]{:S(2)}) async-start(bf16[4,2,2048]{2,1,0:T(2,128)(2,1)} %reshape.38), calls=%async_computation | async-start | bytes 65536 | tf_op jit(solution)/shard_map/all_to_all | solution.py:184
  76.1 6.7 %copy.41 = bf16[2,1,1,8192]{0,2,1,3:T(2,128)(2,1)} copy(bf16[2,1,1,8192]{3,0,2,1:T(2,128)(2,1)S(1)} %get-tuple-element.7) | data formatting | bytes 65536 | tf_op jit(solution)/shard_map/convert_element_type | solution.py:180
  82.9 45.2 %reduce.1 = bf16[8192,2]{1,0:T(8,128)(2,1)S(1)} reduce(bf16[8192,1,1,2]{3,2,1,0:T(2,128)(2,1)} %bitcast.46, bf16[]{:T(256)} %broadcast.2), dimensions={1,2}, to_apply=%bitcast.39.reduce_sub_computation | reduce | bytes 65538
  128.1 3.8 %reshape.40 = bf16[8,2,1024]{2,1,0:T(2,128)(2,1)} reshape(bf16[8192,2]{1,0:T(8,128)(2,1)S(1)} %reduce.1) | data formatting | bytes 65536
  131.9 0.0 all-to-all-done
  132.0 6.5 %all-to-all-start.1 = ((bf16[8,2,1024]{2,1,0:T(2,128)(2,1)}), bf16[8,2,1024]{2,1,0:T(2,128)(2,1)S(1)}, u32[]{:S(2)}, u32[]{:S(2)}) async-start(bf16[8,2,1024]{2,1,0:T(2,128)(2,1)} %reshape.40), calls=%async_computation.1 | async-start | bytes 65536 | tf_op jit(solution)/shard_map/all_to_all | solution.py:185
  138.5 5.9 %reshape.39 = bf16[8192,1,1,2]{3,2,1,0:T(2,128)(2,1)} reshape(bf16[4,2,2048]{2,1,0:T(2,128)(2,1)S(1)} %all-to-all-done) | data formatting | bytes 65536
  144.4 8.1 %copy.40 = bf16[2,1,1,8192]{3,0,2,1:T(2,128)(2,1)S(1)} copy(bf16[2,1,1,8192]{0,2,1,3:T(2,128)(2,1)} %bitcast.47) | data formatting | bytes 65536 | tf_op jit(solution)/shard_map/all_to_all | solution.py:184
  152.5 31.4 %all_gather.6 = bf16[2,4,8,2048]{3,1,0,2:T(4,128)(2,1)S(1)} all-gather(bf16[2,4,1,2048]{3,1,0,2:T(4,128)(2,1)S(1)} %all_to_all.9), channel_id=1, replica_groups=mesh['val'=4,'cond'=8] {'cond'}, dimensions={2}, use_global_device_ids=true | all-gather | bytes 294912 | tf_op jit(solution)/shard_map/all_gather | solution.py:187
  183.9 0.0 all-to-all-done.1
  183.9 6.2 %reshape.41 = bf16[8192,1,1,2]{3,2,1,0:T(2,128)(2,1)} reshape(bf16[8,2,1024]{2,1,0:T(2,128)(2,1)S(1)} %all-to-all-done.1) | data formatting | bytes 65536
  190.1 8.1 %copy.42 = bf16[2,1,1,8192]{3,0,2,1:T(2,128)(2,1)S(1)} copy(bf16[2,1,1,8192]{0,2,1,3:T(2,128)(2,1)} %bitcast.48) | data formatting | bytes 65536 | tf_op jit(solution)/shard_map/all_to_all | solution.py:185
  198.2 5.6 %all_gather.7 = bf16[2,4,8,1024]{3,2,0,1:T(8,128)(2,1)S(1)} all-gather(bf16[2,1,8,1024]{3,2,0,1:T(8,128)(2,1)S(1)} %bitcast.50), channel_id=1, replica_groups=mesh['val'=4,'cond'=8] {'val'}, dimensions={1}, use_global_device_ids=true | all-gather | bytes 163840 | tf_op jit(solution)/shard_map/all_gather | solution.py:186
  203.8 0.1 copy.44
  203.9 0.1 slice_negate_fusion
  204.0 1.4 convolution_bitcast_fusion.1
  205.4 1.4 convolution_bitcast_fusion
  206.8 6.2 %pad_maximum_fusion = f32[2,2048,1024]{2,1,0:T(8,128)} fusion(f32[1,2048,1024]{2,1,0:T(8,128)S(1)} %convolution_bitcast_fusion, f32[1,2048,1024]{2,1,0:T(8,128)S(1)} %convolution_bitcast_fusion.1), kind=kLoop, calls=%fused_computation | loop fusion | flops 4194304 | bytes 33554432 | tf_op jit(solution)/shard_map/stack | solution.py:194
  (2 shorter events, 0.0 us)
Async XLA Ops:
  1.3 1.2 copy-start
  2.5 1.2 copy-start.1
  3.7 0.9 copy-start.2
  4.7 0.8 copy-start.3
  5.5 0.8 copy-start.4
  6.3 0.8 copy-start.5
  71.9 60.0 %all-to-all-start = ((bf16[4,2,2048]{2,1,0:T(2,128)(2,1)}), bf16[4,2,2048]{2,1,0:T(2,128)(2,1)S(1)}, u32[]{:S(2)}, u32[]{:S(2)}) async-start(bf16[4,2,2048]{2,1,0:T(2,128)(2,1)} %reshape.38), calls=%async_computation | async-start | bytes 65536 | tf_op jit(solution)/shard_map/all_to_all | solution.py:184
  132.0 51.9 %all-to-all-start.1 = ((bf16[8,2,1024]{2,1,0:T(2,128)(2,1)}), bf16[8,2,1024]{2,1,0:T(2,128)(2,1)S(1)}, u32[]{:S(2)}, u32[]{:S(2)}) async-start(bf16[8,2,1024]{2,1,0:T(2,128)(2,1)} %reshape.40), calls=%async_computation.1 | async-start | bytes 65536 | tf_op jit(solution)/shard_map/all_to_all | solution.py:185

commit v2 on v1

--- a/solution.py
+++ b/solution.py
@@ -14,6 +14,7 @@
 PAD = 32
 F32 = jnp.float32
 BF16 = jnp.bfloat16
+MESH = pl.DeviceIdType.MESH
 
 
 def reach_of(side, count_g):
@@ -69,13 +70,18 @@
     return results
 
 
-def cube_of(val_ref, cond_ref, along_z, along_y, along_x, val_wide, cond_wide, by_z, by_y, quads):
+def cube_of(
+    ready, weights_ready, val_ref, cond_ref, along_z, along_y, along_x, val_wide, cond_wide, by_z, by_y, quads
+):
     half = SIDE // 2
-    val_wide[...] = val_ref[...].astype(F32)
-    cond_wide[...] = cond_ref[...].astype(F32)
     quarter = SIDE // 4
     for x_high in range(quarter):
         rows = 4 * half
+        if x_high % 4 == 0:
+            ready(x_high // 4)
+        both = slice(2 * rows * x_high, 2 * rows * (x_high + 1))
+        val_wide[both] = val_ref[both].astype(F32)
+        cond_wide[both] = cond_ref[both].astype(F32)
         real_rows = pl.ds(2 * rows * x_high, rows, stride=2)
         imag_rows = pl.ds(2 * rows * x_high + 1, rows, stride=2)
         val_real, val_imag = val_wide[real_rows, :], val_wide[imag_rows, :]
@@ -88,6 +94,7 @@
             pieces = (real_high, imag_high, real_low, imag_low, real_high, imag_high)
             for at, piece in enumerate(pieces):
                 by_z[x_low, there, 128 * at : 128 * (at + 1)] = piece[here]
+    weights_ready()
     lane = lax.broadcasted_iota(jnp.int32, (1, 128), 1) // 32
     step = 128
     for start in range(0, quarter * half, step):
@@ -128,75 +135,247 @@
     return real, imag
 
 
-def density_kernel(reach, val_ref, cond_ref, gvec_ref, wz_ref, wy_ref, wx_ref, out_ref, *scratch):
+def density_kernel(
+    reach,
+    counts,
+    val_ref,
+    cond_ref,
+    gvec_ref,
+    energy_ref,
+    wz_ref,
+    wy_ref,
+    wx_ref,
+    rows_all,
+    cols_all,
+    val_in,
+    cond_in,
+    along_z,
+    along_y,
+    along_x,
+    val_wide,
+    cond_wide,
+    by_z,
+    by_y,
+    cube_ref,
+    row_stage,
+    col_stage,
+    row_send,
+    col_send,
+    in_sems,
+    send_sems,
+    recv_sems,
+):
+    n_val, n_cond = counts
+    val_pos = lax.axis_index("val")
+    cond_pos = lax.axis_index("cond")
+    val_peers = [(lax.rem(val_pos + step, n_val), cond_pos) for step in range(1, n_val)]
+    cond_peers = [(val_pos, lax.rem(cond_pos + step, n_cond)) for step in range(1, n_cond)]
+    barrier = pltpu.get_barrier_semaphore()
+    for peer in val_peers + cond_peers:
+        pl.semaphore_signal(barrier, inc=1, device_id=peer, device_id_type=MESH)
+
+    loads = [
+        pltpu.make_async_copy(source, target, in_sems.at[at])
+        for at, (source, target) in enumerate(
+            ((wz_ref, along_z), (wy_ref, along_y), (wx_ref, along_x))
+        )
+    ]
+    chunks = 4
+    rows = val_in.shape[0] // chunks
+    for chunk in range(chunks):
+        here = slice(rows * chunk, rows * (chunk + 1))
+        loads.append(pltpu.make_async_copy(val_ref.at[here], val_in.at[here], in_sems.at[3 + 2 * chunk]))
+        loads.append(pltpu.make_async_copy(cond_ref.at[here], cond_in.at[here], in_sems.at[4 + 2 * chunk]))
+    for load in loads[3:] + loads[:3]:
+        load.start()
+
+    def ready(chunk):
+        loads[3 + 2 * chunk].wait()
+        loads[4 + 2 * chunk].wait()
+
+    def weights_ready():
+        for load in loads[:3]:
+            load.wait()
+
     quads = (2 * reach + 1 + 3) // 4
-    cube_ref = scratch[-1]
-    cube_ref[...] = cube_of(val_ref, cond_ref, wz_ref, wy_ref, wx_ref, *scratch[:-1], quads)
+    cube_ref[...] = cube_of(
+        ready, weights_ready, val_in, cond_in, along_z, along_y, along_x, val_wide, cond_wide, by_z, by_y, quads
+    )
     step = 512
-
-    @pl.loop(0, out_ref.shape[1] // step)
+    row_lanes, col_lanes = rows_all.shape[3], cols_all.shape[3]
+    count_g = gvec_ref.shape[1]
+    row_segs = count_g // n_val // row_lanes
+    col_segs = count_g // n_cond // col_lanes
+    if row_segs < 8:
+        row_stage[...] = jnp.zeros_like(row_stage)
+    if col_segs < 8:
+        col_stage[...] = jnp.zeros_like(col_stage)
+
+    @pl.loop(0, count_g // step)
     def _(at):
         here = pl.ds(pl.multiple_of(at * step, step), step)
-        real, imag = pick(cube_ref[...], gvec_ref[:, here], reach)
-        out_ref[0:1, here] = real
-        out_ref[1:2, here] = imag
+        picked = pick(cube_ref[...], gvec_ref[:, here], reach)
+        for stage, lanes, segs in ((row_stage, row_lanes, row_segs), (col_stage, col_lanes, col_segs)):
+            for piece in range(step // lanes):
+                whole = at * (step // lanes) + piece
+                for part in range(2):
+                    stage[whole // segs, pl.ds(whole % segs + 8 * part, 1), :] = picked[part][
+                        :, lanes * piece : lanes * (piece + 1)
+                    ]
+
+    total = float(energy_ref.shape[0] * energy_ref.shape[1])
+    weights = -2.0 / (total * energy_ref[...])
+    mine = (lax.broadcasted_iota(jnp.int32, weights.shape, 0) == val_pos) & (
+        lax.broadcasted_iota(jnp.int32, weights.shape, 1) == cond_pos
+    )
+    weight = jnp.sum(jnp.where(mine, weights, 0.0))
+    row_send[...] = (weight * row_stage[...].astype(BF16).astype(F32)).astype(BF16)
+    col_send[...] = col_stage[...].astype(BF16)
+    rows_all[cond_pos, val_pos] = row_send[val_pos]
+    cols_all[cond_pos, val_pos] = col_send[cond_pos]
+
+    def remote(source, target, at, peer):
+        copy = pltpu.make_async_remote_copy(
+            src_ref=source,
+            dst_ref=target,
+            send_sem=send_sems.at[at],
+            recv_sem=recv_sems.at[at],
+            device_id=peer,
+            device_id_type=MESH,
+        )
+        copy.start()
+
+    def wait_for(ref, sem):
+        pltpu.make_async_copy(ref, ref, sem).wait()
+
+    pl.semaphore_wait(barrier, len(val_peers) + len(cond_peers))
+    own = rows_all.at[cond_pos, val_pos]
+    for peer in val_peers:
+        remote(row_send.at[peer[0]], own, 0, peer)
+    own = cols_all.at[cond_pos, val_pos]
+    for peer in cond_peers:
+        remote(col_send.at[peer[1]], own, 1, peer)
+    wait_for(row_send.at[pl.ds(0, n_val - 1)], recv_sems.at[0])
+    own = rows_all.at[cond_pos]
+    for peer in cond_peers:
+        remote(own, own, 2, peer)
+    wait_for(col_send.at[pl.ds(0, n_cond - 1)], recv_sems.at[1])
+    own = cols_all.at[:, val_pos]
+    for peer in val_peers:
+        remote(own, own, 3, peer)
+    for at, ref in (
+        (2, rows_all.at[pl.ds(0, n_cond - 1)]),
+        (3, cols_all.at[:, pl.ds(0, n_val - 1)]),
+    ):
+        wait_for(ref, recv_sems.at[at])
+        wait_for(ref, send_sems.at[at])
+    wait_for(row_send.at[pl.ds(0, n_val - 1)], send_sems.at[0])
+    wait_for(col_send.at[pl.ds(0, n_cond - 1)], send_sems.at[1])
+
+
+def chi_kernel(row_segs, col_segs, rows_all, cols_all, out_ref, row_wide, right):
+    pairs = row_wide.shape[1] // 16
+    lanes = cols_all.shape[1]
+    width = col_segs * lanes
+
+    @pl.when(pl.program_id(0) == 0)
+    def _():
+        for at in range(row_wide.shape[0]):
+            row_wide[at] = rows_all[:, 128 * at : 128 * (at + 1)].astype(F32)
+
+        def with_cols(col_wide):
+            for at in range(lanes // 128):
+                col_wide[...] = cols_all[:, 128 * at : 128 * (at + 1)].astype(F32)
+                for seg in range(col_segs):
+                    real = col_wide[pl.ds(seg, pairs, stride=16), :]
+                    imag = col_wide[pl.ds(seg + 8, pairs, stride=16), :]
+                    start = seg * lanes + 128 * at
+                    here, there = slice(start, start + 128), slice(width + start, width + start + 128)
+                    right[:, here] = jnp.concatenate([real, imag], axis=0).astype(BF16)
+                    right[:, there] = jnp.concatenate([-imag, real], axis=0).astype(BF16)
+
+        pl.run_scoped(with_cols, pltpu.VMEM((cols_all.shape[0], 128), F32))
+
+    seg = pl.program_id(0)
+    tiles = []
+    for at in range(row_wide.shape[0]):
+        real = row_wide[at, pl.ds(seg, pairs, stride=16), :]
+        imag = row_wide[at, pl.ds(seg + 8, pairs, stride=16), :]
+        tiles.append(jnp.concatenate([real, imag], axis=0).T.astype(BF16))
+    left = jnp.concatenate(tiles, axis=0)
+    for part in range(2):
+        out_ref[part] = jnp.dot(
+            left, right[:, width * part : width * (part + 1)], preferred_element_type=F32
+        )
 
 
 def flat_rows(orbital):
     return orbital.reshape(2, -1, 128).transpose(1, 0, 2).reshape(-1, 128)
 
 
-def on_device(orb_val, orb_cond, energies, gvec_map):
+def on_device(counts, orb_val, orb_cond, energies, gvec_map):
+    n_val, n_cond = counts
     count_g = gvec_map.shape[0]
     reach = reach_of(SIDE, count_g)
-    along_z, along_y, along_x = dft_matrices(reach)
+    matrices = [jnp.asarray(m) for m in dft_matrices(reach)]
     rows = 2 * SIDE**3 // 128
     quads = (2 * reach + 1 + 3) // 4
-    dense = pl.pallas_call(
-        functools.partial(density_kernel, reach),
-        out_shape=jax.ShapeDtypeStruct((2, count_g), F32),
-        in_specs=[pl.BlockSpec(memory_space=pltpu.VMEM)] * 6,
-        out_specs=pl.BlockSpec(memory_space=pltpu.VMEM),
+    row_block, col_block = count_g // n_val, count_g // n_cond
+    row_lanes, col_lanes = max(128, row_block // 8), max(128, col_block // 8)
+    row_segs, col_segs = row_block // row_lanes, col_block // col_lanes
+    vmem = pl.BlockSpec(memory_space=pltpu.VMEM)
+    anywhere = pl.BlockSpec(memory_space=pl.ANY)
+    rows_all, cols_all = pl.pallas_call(
+        functools.partial(density_kernel, reach, counts),
+        out_shape=[
+            jax.ShapeDtypeStruct((n_cond, n_val, 16, row_lanes), BF16),
+            jax.ShapeDtypeStruct((n_cond, n_val, 16, col_lanes), BF16),
+        ],
+        in_specs=[anywhere, anywhere, vmem, vmem, anywhere, anywhere, anywhere],
+        out_specs=[vmem, vmem],
         scratch_shapes=[
+            pltpu.VMEM((rows, 128), BF16),
+            pltpu.VMEM((rows, 128), BF16),
+            pltpu.VMEM(matrices[0].shape, BF16),
+            pltpu.VMEM(matrices[1].shape, BF16),
+            pltpu.VMEM(matrices[2].shape, BF16),
             pltpu.VMEM((rows, 128), F32),
             pltpu.VMEM((rows, 128), F32),
             pltpu.VMEM((4, SIDE // 4 * SIDE // 2, 6 * 128), BF16),
             pltpu.VMEM((SIDE * PAD, 128), F32),
             pltpu.VMEM((2 * PAD, 128 * quads), BF16),
+            pltpu.VMEM((n_val, 16, row_lanes), F32),
+            pltpu.VMEM((n_cond, 16, col_lanes), F32),
+            pltpu.VMEM((n_val, 16, row_lanes), BF16),
+            pltpu.VMEM((n_cond, 16, col_lanes), BF16),
+            pltpu.SemaphoreType.DMA((11,)),
+            pltpu.SemaphoreType.DMA((4,)),
+            pltpu.SemaphoreType.DMA((4,)),
+        ],
+        compiler_params=pltpu.CompilerParams(
+            vmem_limit_bytes=48 * 2**20, collective_id=0, has_side_effects=True
+        ),
+        name="density",
+    )(flat_rows(orb_val), flat_rows(orb_cond), gvec_map.reshape(1, count_g), energies, *matrices)
+    high = n_cond * n_val * 16
+    return pl.pallas_call(
+        functools.partial(chi_kernel, row_segs, col_segs),
+        grid=(row_segs,),
+        out_shape=jax.ShapeDtypeStruct((2, row_block, col_block), F32),
+        in_specs=[vmem, vmem],
+        out_specs=pl.BlockSpec((2, row_lanes, col_block), lambda seg: (0, seg, 0)),
+        scratch_shapes=[
+            pltpu.VMEM((row_lanes // 128, high, 128), F32),
+            pltpu.VMEM((high // 8, 2 * col_block), BF16),
         ],
         compiler_params=pltpu.CompilerParams(vmem_limit_bytes=48 * 2**20),
-        name="density",
-    )(
-        flat_rows(orb_val),
-        flat_rows(orb_cond),
-        gvec_map.reshape(1, count_g),
-        jnp.asarray(along_z),
-        jnp.asarray(along_y),
-        jnp.asarray(along_x),
-    )
-    total_val, total_cond = energies.shape
-    val_pos = lax.axis_index("val")
-    cond_pos = lax.axis_index("cond")
-    density = dense[:, None, None, :].astype(BF16)
-    weight_all = -2.0 / (float(total_val * total_cond) * energies)
-    weight_local = lax.dynamic_slice(weight_all, (val_pos, cond_pos), (1, 1))
-    weighted = (weight_local[None, :, :, None] * density.astype(F32)).astype(BF16)
-    rows = lax.all_to_all(weighted, "val", split_axis=3, concat_axis=1, tiled=True)
-    col_part = lax.all_to_all(density, "cond", split_axis=3, concat_axis=2, tiled=True)
-    cols = lax.all_gather(col_part, "val", axis=1, tiled=True)
-    rows_all = lax.all_gather(rows, "cond", axis=2, tiled=True)
-    left = rows_all.reshape(-1, rows_all.shape[3])
-    right = cols.reshape(-1, cols.shape[3])
-    turned = jnp.concatenate([-cols[1:2], cols[0:1]], axis=0).reshape(-1, cols.shape[3])
-    dims = (((0,), (0,)), ((), ()))
-    real_sum = lax.dot_general(left, right, dims, preferred_element_type=F32)
-    imag_sum = lax.dot_general(left, turned, dims, preferred_element_type=F32)
-    return jnp.stack([real_sum, imag_sum])
+        name="chi",
+    )(rows_all.reshape(high, row_lanes), cols_all.reshape(high, col_lanes))
 
 
 def solution(mesh):
     return jax.shard_map(
-        on_device,
+        functools.partial(on_device, (mesh.shape["val"], mesh.shape["cond"])),
         mesh=mesh,
         in_specs=(P(None, "val", None), P(None, "cond", None), P(), P()),
         out_specs=P(None, "val", "cond"),

time: 214 us -> 37.2 us (0.17)
  other arithmetic: 98.2 us -> 0 us
  local copies, waits for them, and re-layouts: 56.5 us -> 6.41 us
  blocking collectives: 37 us -> 0 us
  Pallas kernels: 7.77 us -> 30.4 us
  starting transfers between devices: 10.8 us -> 0 us
  matrix products: 2.82 us -> 0 us
    unnamed x2 -> x0, other arithmetic: 90.5 us -> none
    all_gather x2 -> x0, blocking collectives: 37 us -> none  [the longest x1 31.4 us: on_device(): rows_all = lax.all_gather(rows, 'cond', axis=2, tiled=True)]
    pallas_call x1 -> x2, Pallas kernels: 7.77 us -> 30.4 us  [the longest x1 22.3 us: on_device(): pl.pallas_call(functools.partial(density_kernel, reach, counts), out_shap...]
    unnamed x18 -> x14, local copies, waits for them, and re-layouts: 26.1 us -> 6.41 us
    all_to_all x3 -> x0, local copies, waits for them, and re-layouts: 16.2 us -> none  [the longest x2 8.1 us: on_device(): lax.all_to_all(weighted, 'val', split_axis=3, concat_axis=1, tiled=True)]
    convert_element_type x2 -> x0, local copies, waits for them, and re-layouts: 13.5 us -> none  [the longest x1 6.76 us: on_device(): (weight_local[None, :, :, None] * density.astype(F32)).astype(BF16)]
    all_to_all x2 -> x0, starting transfers between devices: 10.8 us -> none  [the longest x1 6.51 us: on_device(): lax.all_to_all(density, 'cond', split_axis=3, concat_axis=2, tiled=True)]
    another operation x1 -> x0, other arithmetic: 6.25 us -> none  [on_device(): return jnp.stack([real_sum, imag_sum])]
  transfers between devices with their start and end apart: 2 -> 0, of which waited for: 0 -> 0; matrix products, arithmetic and copies ran while one was open for 33% -> 0% of each run, Pallas kernels for 0% -> 0%
where the time goes in v2:
time: 37.2 us; the launch traced here: 36.8 us
  Pallas kernels  30.4 us (82%)
  local copies, waits for them, and re-layouts  6.41 us (17%)
    pallas_call x1, Pallas kernels, on_device(): pl.pallas_call(functools.partial(density_kernel, reach, counts), out_shap...  22.3 us
    pallas_call x1, Pallas kernels, on_device(): pl.pallas_call(functools.partial(chi_kernel, row_segs, col_segs), grid=(r...  8.08 us
    unnamed x14, local copies, waits for them, and re-layouts  6.41 us

profile of v2, /device:TPU:0, one launch (start us, length us, event | category | flops | bytes accessed | tf_op | source)
XLA Modules:
  0.0 36.8 jit_solution(135640281961514292)
XLA Ops:
  0.0 0.0 copy-start
  0.0 1.2 %copy-done = bf16[2,1,262144]{2,0,1:T(2,128)(2,1)S(1)} copy-done((bf16[2,1,262144]{2,0,1:T(2,128)(2,1)S(1)}, bf16[2,1,262144]{2,0,1:T(2,128)(2,1)}, u32[]{:S(2)}) %copy-start) | copy-done | bytes 1048600
  1.2 0.0 copy-start.1
  1.2 1.2 %copy-done.1 = bf16[2,1,262144]{2,0,1:T(2,128)(2,1)S(1)} copy-done((bf16[2,1,262144]{2,0,1:T(2,128)(2,1)S(1)}, bf16[2,1,262144]{2,0,1:T(2,128)(2,1)}, u32[]{:S(2)}) %copy-start.1) | copy-done | bytes 1048600
  2.5 0.0 copy-start.2
  2.5 0.9 %copy-done.2 = bf16[768,128]{1,0:T(8,128)(2,1)S(1)} copy-done((bf16[768,128]{1,0:T(8,128)(2,1)S(1)}, bf16[768,128]{1,0:T(8,128)(2,1)}, u32[]{:S(2)}) %copy-start.2) | copy-done | bytes 196632
  3.4 0.0 copy-start.3
  3.4 0.8 %copy-done.3 = bf16[64,384]{1,0:T(8,128)(2,1)S(1)} copy-done((bf16[64,384]{1,0:T(8,128)(2,1)S(1)}, bf16[64,384]{1,0:T(8,128)(2,1)}, u32[]{:S(2)}) %copy-start.3) | copy-done | bytes 49176
  4.2 0.0 copy-start.4
  4.2 0.8 %copy-done.4 = bf16[64,384]{1,0:T(8,128)(2,1)S(1)} copy-done((bf16[64,384]{1,0:T(8,128)(2,1)S(1)}, bf16[64,384]{1,0:T(8,128)(2,1)}, u32[]{:S(2)}) %copy-start.4) | copy-done | bytes 49176
  5.0 0.0 copy-start.5
  5.0 0.8 %copy-done.5 = s32[8192]{0:T(1024)S(1)} copy-done((s32[8192]{0:T(1024)S(1)}, s32[8192]{0:T(1024)}, u32[]{:S(2)}) %copy-start.5) | copy-done | bytes 32792
  5.7 0.0 copy-start.6
  5.7 0.7 %copy-done.6 = f32[4,8]{1,0:T(4,128)S(1)} copy-done((f32[4,8]{1,0:T(4,128)S(1)}, f32[4,8]{1,0:T(4,128)}, u32[]{:S(2)}) %copy-start.6) | copy-done | bytes 152
  6.4 22.3 %density.1 = (bf16[8,4,16,256]{3,2,1,0:T(8,128)(2,1)S(1)}, bf16[8,4,16,128]{3,2,1,0:T(8,128)(2,1)S(1)}) custom-call(bf16[4096,128]{1,0:T(8,128)(2,1)S(1)} %bitcast.13, bf16[4096,128]{1,0:T(8,128)(2,1)S(1)} %bitcast.14, s32[1,8192]{1,0:T(1,128)S(1)} %bitcast.17, f32[4,8]{1,0:T(4,128)S(1)} %copy-done.6, bf16[768,128]{1,0:T(8,128)(2,1)S(1)} %copy-done.2, ...), custom_call_target="tpu_custom_call" | custom-call | tf_op jit(solution)/shard_map/density/pallas_call | solution.py:328
  28.8 8.1 %chi.1 = f32[2,2048,1024]{2,1,0:T(8,128)} custom-call(bf16[512,256]{1,0:T(8,128)(2,1)S(1)} %bitcast.15, bf16[512,128]{1,0:T(8,128)(2,1)S(1)} %bitcast.16), custom_call_target="tpu_custom_call" | custom-call | tf_op jit(solution)/shard_map/chi/pallas_call | solution.py:361
Async XLA Ops:
  0.0 1.2 %copy-start = (bf16[2,1,262144]{2,0,1:T(2,128)(2,1)S(1)}, bf16[2,1,262144]{2,0,1:T(2,128)(2,1)}, u32[]{:S(2)}) copy-start(bf16[2,1,262144]{2,0,1:T(2,128)(2,1)} %param.7) | copy-start | bytes 3145732
  1.2 1.2 %copy-start.1 = (bf16[2,1,262144]{2,0,1:T(2,128)(2,1)S(1)}, bf16[2,1,262144]{2,0,1:T(2,128)(2,1)}, u32[]{:S(2)}) copy-start(bf16[2,1,262144]{2,0,1:T(2,128)(2,1)} %param.8) | copy-start | bytes 3145732
  2.5 0.9 %copy-start.2 = (bf16[768,128]{1,0:T(8,128)(2,1)S(1)}, bf16[768,128]{1,0:T(8,128)(2,1)}, u32[]{:S(2)}) copy-start(bf16[768,128]{1,0:T(8,128)(2,1)} %constant.6.clone.wz_ref) | copy-start | bytes 589828
  3.4 0.8 %copy-start.3 = (bf16[64,384]{1,0:T(8,128)(2,1)S(1)}, bf16[64,384]{1,0:T(8,128)(2,1)}, u32[]{:S(2)}) copy-start(bf16[64,384]{1,0:T(8,128)(2,1)} %constant.8.clone.wx_ref) | copy-start | bytes 147460
  4.2 0.8 %copy-start.4 = (bf16[64,384]{1,0:T(8,128)(2,1)S(1)}, bf16[64,384]{1,0:T(8,128)(2,1)}, u32[]{:S(2)}) copy-start(bf16[64,384]{1,0:T(8,128)(2,1)} %constant.7.clone.wy_ref) | copy-start | bytes 147460
  5.0 0.8 %copy-start.5 = (s32[8192]{0:T(1024)S(1)}, s32[8192]{0:T(1024)}, u32[]{:S(2)}) copy-start(s32[8192]{0:T(1024)} %param.10) | copy-start | bytes 98308
  5.7 0.7 %copy-start.6 = (f32[4,8]{1,0:T(4,128)S(1)}, f32[4,8]{1,0:T(4,128)}, u32[]{:S(2)}) copy-start(f32[4,8]{1,0:T(4,128)} %energy_ref.1) | copy-start | bytes 388

commit v3 on v2

--- a/solution.py
+++ b/solution.py
@@ -140,8 +140,8 @@
     counts,
     val_ref,
     cond_ref,
-    gvec_ref,
-    energy_ref,
+    gvec_in,
+    energy_in,
     wz_ref,
     wy_ref,
     wx_ref,
@@ -149,6 +149,8 @@
     cols_all,
     val_in,
     cond_in,
+    gvec_ref,
+    energy_ref,
     along_z,
     along_y,
     along_x,
@@ -177,100 +179,135 @@
     loads = [
         pltpu.make_async_copy(source, target, in_sems.at[at])
         for at, (source, target) in enumerate(
-            ((wz_ref, along_z), (wy_ref, along_y), (wx_ref, along_x))
+            (
+                (wz_ref, along_z),
+                (wy_ref, along_y),
+                (wx_ref, along_x),
+                (gvec_in, gvec_ref),
+                (energy_in, energy_ref),
+            )
         )
     ]
     chunks = 4
     rows = val_in.shape[0] // chunks
     for chunk in range(chunks):
         here = slice(rows * chunk, rows * (chunk + 1))
-        loads.append(pltpu.make_async_copy(val_ref.at[here], val_in.at[here], in_sems.at[3 + 2 * chunk]))
-        loads.append(pltpu.make_async_copy(cond_ref.at[here], cond_in.at[here], in_sems.at[4 + 2 * chunk]))
-    for load in loads[3:] + loads[:3]:
+        loads.append(pltpu.make_async_copy(val_ref.at[here], val_in.at[here], in_sems.at[5 + 2 * chunk]))
+        loads.append(pltpu.make_async_copy(cond_ref.at[here], cond_in.at[here], in_sems.at[6 + 2 * chunk]))
+    for load in loads[5:] + loads[:5]:
         load.start()
 
     def ready(chunk):
-        loads[3 + 2 * chunk].wait()
-        loads[4 + 2 * chunk].wait()
+        loads[5 + 2 * chunk].wait()
+        loads[6 + 2 * chunk].wait()
 
     def weights_ready():
-        for load in loads[:3]:
+        for load in loads[:5]:
             load.wait()
 
     quads = (2 * reach + 1 + 3) // 4
     cube_ref[...] = cube_of(
         ready, weights_ready, val_in, cond_in, along_z, along_y, along_x, val_wide, cond_wide, by_z, by_y, quads
     )
-    step = 512
-    row_lanes, col_lanes = rows_all.shape[3], cols_all.shape[3]
-    count_g = gvec_ref.shape[1]
-    row_segs = count_g // n_val // row_lanes
-    col_segs = count_g // n_cond // col_lanes
-    if row_segs < 8:
-        row_stage[...] = jnp.zeros_like(row_stage)
-    if col_segs < 8:
-        col_stage[...] = jnp.zeros_like(col_stage)
-
-    @pl.loop(0, count_g // step)
-    def _(at):
-        here = pl.ds(pl.multiple_of(at * step, step), step)
-        picked = pick(cube_ref[...], gvec_ref[:, here], reach)
-        for stage, lanes, segs in ((row_stage, row_lanes, row_segs), (col_stage, col_lanes, col_segs)):
-            for piece in range(step // lanes):
-                whole = at * (step // lanes) + piece
-                for part in range(2):
-                    stage[whole // segs, pl.ds(whole % segs + 8 * part, 1), :] = picked[part][
-                        :, lanes * piece : lanes * (piece + 1)
-                    ]
-
     total = float(energy_ref.shape[0] * energy_ref.shape[1])
     weights = -2.0 / (total * energy_ref[...])
     mine = (lax.broadcasted_iota(jnp.int32, weights.shape, 0) == val_pos) & (
         lax.broadcasted_iota(jnp.int32, weights.shape, 1) == cond_pos
     )
     weight = jnp.sum(jnp.where(mine, weights, 0.0))
-    row_send[...] = (weight * row_stage[...].astype(BF16).astype(F32)).astype(BF16)
-    col_send[...] = col_stage[...].astype(BF16)
-    rows_all[cond_pos, val_pos] = row_send[val_pos]
-    cols_all[cond_pos, val_pos] = col_send[cond_pos]
-
-    def remote(source, target, at, peer):
-        copy = pltpu.make_async_remote_copy(
+
+    row_lanes, col_lanes = rows_all.shape[3], cols_all.shape[3]
+    count_g = gvec_ref.shape[1]
+    row_block = count_g // n_val
+    row_segs = row_block // row_lanes
+    col_segs = count_g // n_cond // col_lanes
+    ratio = n_cond // n_val
+    step = min(512, row_block)
+    if row_segs < 8:
+        row_stage[...] = jnp.zeros_like(row_stage)
+    if col_segs < 8:
+        col_stage[...] = jnp.zeros_like(col_stage)
+
+    def gather(block):
+        @pl.loop(0, row_block // step)
+        def _(at):
+            start = block * row_block + at * step
+            picked = pick(cube_ref[...], gvec_ref[:, pl.ds(pl.multiple_of(start, step), step)], reach)
+            for stage, lanes, segs in ((row_stage, row_lanes, row_segs), (col_stage, col_lanes, col_segs)):
+                for piece in range(step // lanes):
+                    whole = at * (step // lanes) + piece
+                    for part in range(2):
+                        stage[whole // segs, pl.ds(whole % segs + 8 * part, 1), :] = picked[part][
+                            :, lanes * piece : lanes * (piece + 1)
+                        ]
+
+    def remote(source, target, sems, peer):
+        pltpu.make_async_remote_copy(
             src_ref=source,
             dst_ref=target,
-            send_sem=send_sems.at[at],
-            recv_sem=recv_sems.at[at],
+            send_sem=sems[0],
+            recv_sem=sems[1],
             device_id=peer,
             device_id_type=MESH,
-        )
-        copy.start()
+        ).start()
 
     def wait_for(ref, sem):
         pltpu.make_async_copy(ref, ref, sem).wait()
 
-    pl.semaphore_wait(barrier, len(val_peers) + len(cond_peers))
-    own = rows_all.at[cond_pos, val_pos]
-    for peer in val_peers:
-        remote(row_send.at[peer[0]], own, 0, peer)
-    own = cols_all.at[cond_pos, val_pos]
-    for peer in cond_peers:
-        remote(col_send.at[peer[1]], own, 1, peer)
-    wait_for(row_send.at[pl.ds(0, n_val - 1)], recv_sems.at[0])
-    own = rows_all.at[cond_pos]
-    for peer in cond_peers:
-        remote(own, own, 2, peer)
-    wait_for(col_send.at[pl.ds(0, n_cond - 1)], recv_sems.at[1])
+    col_sems = (send_sems.at[0], recv_sems.at[0])
+    col_late = (send_sems.at[1], recv_sems.at[1])
+    row_late = (send_sems.at[2], recv_sems.at[2])
+
+    def spread(val_from):
+        piece = rows_all.at[cond_pos, val_from]
+        for peer in cond_peers:
+            remote(piece, piece, row_late, peer)
+
+    def arrived(distance):
+        wait_for(row_send.at[0], recv_sems.at[3 + distance])
+        spread(lax.rem(val_pos + n_val - distance, n_val))
+
+    for distance in range(n_val):
+        block = lax.rem(val_pos + distance, n_val)
+        gather(block)
+        if distance == 0:
+            pl.semaphore_wait(barrier, len(val_peers) + len(cond_peers))
+        ready_rows = (weight * row_stage[0].astype(BF16).astype(F32)).astype(BF16)
+        if distance == 0:
+            rows_all[cond_pos, val_pos] = ready_rows
+            spread(val_pos)
+        else:
+            row_send[distance - 1] = ready_rows
+            own = rows_all.at[cond_pos, val_pos]
+            sems = (send_sems.at[3 + distance], recv_sems.at[3 + distance])
+            remote(row_send.at[distance - 1], own, sems, (block, cond_pos))
+        for at in range(ratio):
+            target = block * ratio + at
+            col_send[target] = col_stage[at].astype(BF16)
+
+            @pl.when(target != cond_pos)
+            def _():
+                own = cols_all.at[cond_pos, val_pos]
+                remote(col_send.at[target], own, col_sems, (val_pos, target))
+
+        if distance > 1:
+            arrived(distance - 1)
+    cols_all[cond_pos, val_pos] = col_send[cond_pos]
+    if n_val > 1:
+        arrived(n_val - 1)
+    wait_for(col_send.at[pl.ds(0, n_cond - 1)], col_sems[1])
     own = cols_all.at[:, val_pos]
     for peer in val_peers:
-        remote(own, own, 3, peer)
-    for at, ref in (
-        (2, rows_all.at[pl.ds(0, n_cond - 1)]),
-        (3, cols_all.at[:, pl.ds(0, n_val - 1)]),
+        remote(own, own, col_late, peer)
+    for ref, sems in (
+        (rows_all.at[pl.ds(0, n_cond - 1)], row_late),
+        (cols_all.at[:, pl.ds(0, n_val - 1)], col_late),
     ):
-        wait_for(ref, recv_sems.at[at])
-        wait_for(ref, send_sems.at[at])
-    wait_for(row_send.at[pl.ds(0, n_val - 1)], send_sems.at[0])
-    wait_for(col_send.at[pl.ds(0, n_cond - 1)], send_sems.at[1])
+        wait_for(ref, sems[1])
+        wait_for(ref, sems[0])
+    for distance in range(1, n_val):
+        wait_for(row_send.at[0], send_sems.at[3 + distance])
+    wait_for(col_send.at[pl.ds(0, n_cond - 1)], col_sems[0])
 
 
 def chi_kernel(row_segs, col_segs, rows_all, cols_all, out_ref, row_wide, right):
@@ -324,18 +361,20 @@
     row_lanes, col_lanes = max(128, row_block // 8), max(128, col_block // 8)
     row_segs, col_segs = row_block // row_lanes, col_block // col_lanes
     vmem = pl.BlockSpec(memory_space=pltpu.VMEM)
-    anywhere = pl.BlockSpec(memory_space=pl.ANY)
+    hbm = pl.BlockSpec(memory_space=pltpu.HBM)
     rows_all, cols_all = pl.pallas_call(
         functools.partial(density_kernel, reach, counts),
         out_shape=[
             jax.ShapeDtypeStruct((n_cond, n_val, 16, row_lanes), BF16),
             jax.ShapeDtypeStruct((n_cond, n_val, 16, col_lanes), BF16),
         ],
-        in_specs=[anywhere, anywhere, vmem, vmem, anywhere, anywhere, anywhere],
+        in_specs=[hbm] * 7,
         out_specs=[vmem, vmem],
         scratch_shapes=[
             pltpu.VMEM((rows, 128), BF16),
             pltpu.VMEM((rows, 128), BF16),
+            pltpu.VMEM((1, count_g), jnp.int32),
+            pltpu.VMEM(energies.shape, F32),
             pltpu.VMEM(matrices[0].shape, BF16),
             pltpu.VMEM(matrices[1].shape, BF16),
             pltpu.VMEM(matrices[2].shape, BF16),
@@ -344,16 +383,16 @@
             pltpu.VMEM((4, SIDE // 4 * SIDE // 2, 6 * 128), BF16),
             pltpu.VMEM((SIDE * PAD, 128), F32),
             pltpu.VMEM((2 * PAD, 128 * quads), BF16),
-            pltpu.VMEM((n_val, 16, row_lanes), F32),
-            pltpu.VMEM((n_cond, 16, col_lanes), F32),
+            pltpu.VMEM((1, 16, row_lanes), F32),
+            pltpu.VMEM((n_cond // n_val, 16, col_lanes), F32),
             pltpu.VMEM((n_val, 16, row_lanes), BF16),
             pltpu.VMEM((n_cond, 16, col_lanes), BF16),
-            pltpu.SemaphoreType.DMA((11,)),
-            pltpu.SemaphoreType.DMA((4,)),
-            pltpu.SemaphoreType.DMA((4,)),
+            pltpu.SemaphoreType.DMA((13,)),
+            pltpu.SemaphoreType.DMA((3 + n_val,)),
+            pltpu.SemaphoreType.DMA((3 + n_val,)),
         ],
         compiler_params=pltpu.CompilerParams(
-            vmem_limit_bytes=48 * 2**20, collective_id=0, has_side_effects=True
+            vmem_limit_bytes=62 * 2**20, collective_id=0, has_side_effects=True
         ),
         name="density",
     )(flat_rows(orb_val), flat_rows(orb_cond), gvec_map.reshape(1, count_g), energies, *matrices)

time: 37.2 us -> 30.9 us (0.83)
  local copies, waits for them, and re-layouts: 6.41 us -> 1.85 us
  Pallas kernels: 30.4 us -> 28.9 us
    unnamed x14 -> x4, local copies, waits for them, and re-layouts: 6.41 us -> 1.85 us
    pallas_call x1, Pallas kernels: 22.3 us -> 20.8 us  [on_device(): pl.pallas_call(functools.partial(density_kernel, reach, counts), out_shap...]
where the time goes in v3:
time: 30.9 us; the launch traced here: 30.8 us
  Pallas kernels  28.9 us (94%)
  local copies, waits for them, and re-layouts  1.85 us (6%)
    pallas_call x1, Pallas kernels, on_device(): pl.pallas_call(functools.partial(density_kernel, reach, counts), out_shap...  20.8 us
    pallas_call x1, Pallas kernels, on_device(): pl.pallas_call(functools.partial(chi_kernel, row_segs, col_segs), grid=(r...  8.06 us
    unnamed x4, local copies, waits for them, and re-layouts  1.85 us

profile of v3, /device:TPU:0, one launch (start us, length us, event | category | flops | bytes accessed | tf_op | source)
XLA Modules:
  0.0 30.8 jit_solution(7759257687800595129)
XLA Ops:
  0.0 20.8 %density.1 = (bf16[8,4,16,256]{3,2,1,0:T(8,128)(2,1)}, bf16[8,4,16,128]{3,2,1,0:T(8,128)(2,1)}) custom-call(bf16[4096,128]{1,0:T(8,128)(2,1)} %bitcast.15, bf16[4096,128]{1,0:T(8,128)(2,1)} %bitcast.16, s32[1,8192]{1,0:T(1,128)} %bitcast.17, f32[4,8]{1,0:T(4,128)} %energy_in.1, bf16[768,128]{1,0:T(8,128)(2,1)} %constant.6.clone.wz_ref, ...), custom_call_target="tpu_custom_call" | custom-call | tf_op jit(solution)/shard_map/density/pallas_call | solution.py:365
  20.9 0.0 copy-start
  20.9 0.9 %copy-done = bf16[8,4,16,256]{3,2,1,0:T(8,128)(2,1)S(1)} copy-done((bf16[8,4,16,256]{3,2,1,0:T(8,128)(2,1)S(1)}, bf16[8,4,16,256]{3,2,1,0:T(8,128)(2,1)}, u32[]{:S(2)}) %copy-start) | copy-done | bytes 262168
  21.8 0.0 copy-start.1
  21.8 0.9 %copy-done.1 = bf16[8,4,16,128]{3,2,1,0:T(8,128)(2,1)S(1)} copy-done((bf16[8,4,16,128]{3,2,1,0:T(8,128)(2,1)S(1)}, bf16[8,4,16,128]{3,2,1,0:T(8,128)(2,1)}, u32[]{:S(2)}) %copy-start.1) | copy-done | bytes 131096
  22.7 8.1 %chi.1 = f32[2,2048,1024]{2,1,0:T(8,128)} custom-call(bf16[512,256]{1,0:T(8,128)(2,1)S(1)} %bitcast.13, bf16[512,128]{1,0:T(8,128)(2,1)S(1)} %bitcast.14), custom_call_target="tpu_custom_call" | custom-call | tf_op jit(solution)/shard_map/chi/pallas_call | solution.py:400
Async XLA Ops:
  20.9 1.0 %copy-start = (bf16[8,4,16,256]{3,2,1,0:T(8,128)(2,1)S(1)}, bf16[8,4,16,256]{3,2,1,0:T(8,128)(2,1)}, u32[]{:S(2)}) copy-start(bf16[8,4,16,256]{3,2,1,0:T(8,128)(2,1)} %get-tuple-element.7) | copy-start | bytes 786436
  21.8 0.9 %copy-start.1 = (bf16[8,4,16,128]{3,2,1,0:T(8,128)(2,1)S(1)}, bf16[8,4,16,128]{3,2,1,0:T(8,128)(2,1)}, u32[]{:S(2)}) copy-start(bf16[8,4,16,128]{3,2,1,0:T(8,128)(2,1)} %get-tuple-element.8) | copy-start | bytes 393220

commit v4 on v3

--- a/solution.py
+++ b/solution.py
@@ -127,7 +127,8 @@
     z_pos = (cells + reach) & (SIDE - 1)
     place = z_pos * PAD + y_pos
     rows = lax.broadcasted_iota(jnp.int32, (cube.shape[1], count), 0)
-    chosen = jnp.where(rows == place, 1.0, 0.0).astype(BF16)
+    hit = rows.astype(jnp.int16) == place.astype(jnp.int16)
+    chosen = jnp.where(hit, jnp.ones((), BF16), jnp.zeros((), BF16))
     lines = jnp.dot(cube, chosen, preferred_element_type=F32)
     plane = lax.broadcasted_iota(jnp.int32, (PAD, count), 0) == x_pos
     real = jnp.sum(jnp.where(plane, lines[:PAD], 0.0), axis=0, keepdims=True)
@@ -166,6 +167,7 @@
     in_sems,
     send_sems,
     recv_sems,
+    far_sems,
 ):
     n_val, n_cond = counts
     val_pos = lax.axis_index("val")
@@ -258,14 +260,30 @@
     col_late = (send_sems.at[1], recv_sems.at[1])
     row_late = (send_sems.at[2], recv_sems.at[2])
 
-    def spread(val_from):
-        piece = rows_all.at[cond_pos, val_from]
-        for peer in cond_peers:
-            remote(piece, piece, row_late, peer)
+    n_far = n_cond // 2
+    far, near = cond_pos // 2, lax.rem(cond_pos, 2)
+    partner = (val_pos, far * 2 + 1 - near)
+
+    def source_of(distance):
+        return lax.rem(val_pos + n_val - distance, n_val)
+
+    def spread(distance):
+        piece = rows_all.at[cond_pos, source_of(distance)]
+        for hop in range(1, n_far):
+            peer = (val_pos, lax.rem(far + hop, n_far) * 2 + near)
+            remote(piece, piece, (send_sems.at[2], far_sems.at[hop, distance]), peer)
+        remote(piece, piece, row_late, partner)
 
     def arrived(distance):
         wait_for(row_send.at[0], recv_sems.at[3 + distance])
-        spread(lax.rem(val_pos + n_val - distance, n_val))
+        spread(distance)
+
+    def forward(distance):
+        for hop in range(1, n_far):
+            wait_for(row_send.at[0], far_sems.at[hop, distance])
+            origin = lax.rem(far + n_far - hop, n_far) * 2 + near
+            piece = rows_all.at[origin, source_of(distance)]
+            remote(piece, piece, row_late, partner)
 
     for distance in range(n_val):
         block = lax.rem(val_pos + distance, n_val)
@@ -275,7 +293,7 @@
         ready_rows = (weight * row_stage[0].astype(BF16).astype(F32)).astype(BF16)
         if distance == 0:
             rows_all[cond_pos, val_pos] = ready_rows
-            spread(val_pos)
+            spread(0)
         else:
             row_send[distance - 1] = ready_rows
             own = rows_all.at[cond_pos, val_pos]
@@ -292,6 +310,10 @@
 
         if distance > 1:
             arrived(distance - 1)
+        if distance == 1:
+            forward(0)
+        if distance > 2:
+            forward(distance - 2)
     cols_all[cond_pos, val_pos] = col_send[cond_pos]
     if n_val > 1:
         arrived(n_val - 1)
@@ -299,26 +321,32 @@
     own = cols_all.at[:, val_pos]
     for peer in val_peers:
         remote(own, own, col_late, peer)
-    for ref, sems in (
-        (rows_all.at[pl.ds(0, n_cond - 1)], row_late),
-        (cols_all.at[:, pl.ds(0, n_val - 1)], col_late),
-    ):
-        wait_for(ref, sems[1])
-        wait_for(ref, sems[0])
+    if n_val > 2:
+        forward(n_val - 2)
+    if n_val > 1:
+        forward(n_val - 1)
+    wait_for(rows_all.at[pl.ds(0, n_far)], row_late[1])
+    wait_for(rows_all.at[pl.ds(0, n_cond - 1)], row_late[0])
+    late = cols_all.at[:, pl.ds(0, n_val - 1)]
+    wait_for(late, col_late[1])
+    wait_for(late, col_late[0])
     for distance in range(1, n_val):
         wait_for(row_send.at[0], send_sems.at[3 + distance])
     wait_for(col_send.at[pl.ds(0, n_cond - 1)], col_sems[0])
 
 
-def chi_kernel(row_segs, col_segs, rows_all, cols_all, out_ref, row_wide, right):
+def chi_kernel(col_segs, rows_hbm, cols_hbm, out_ref, rows_all, cols_all, row_wide, right, sems):
     pairs = row_wide.shape[1] // 16
     lanes = cols_all.shape[1]
     width = col_segs * lanes
 
     @pl.when(pl.program_id(0) == 0)
     def _():
-        for at in range(row_wide.shape[0]):
-            row_wide[at] = rows_all[:, 128 * at : 128 * (at + 1)].astype(F32)
+        cols_load = pltpu.make_async_copy(cols_hbm, cols_all, sems.at[0])
+        rows_load = pltpu.make_async_copy(rows_hbm, rows_all, sems.at[1])
+        cols_load.start()
+        rows_load.start()
+        cols_load.wait()
 
         def with_cols(col_wide):
             for at in range(lanes // 128):
@@ -332,6 +360,9 @@
                     right[:, there] = jnp.concatenate([-imag, real], axis=0).astype(BF16)
 
         pl.run_scoped(with_cols, pltpu.VMEM((cols_all.shape[0], 128), F32))
+        rows_load.wait()
+        for at in range(row_wide.shape[0]):
+            row_wide[at] = rows_all[:, 128 * at : 128 * (at + 1)].astype(F32)
 
     seg = pl.program_id(0)
     tiles = []
@@ -390,6 +421,7 @@
             pltpu.SemaphoreType.DMA((13,)),
             pltpu.SemaphoreType.DMA((3 + n_val,)),
             pltpu.SemaphoreType.DMA((3 + n_val,)),
+            pltpu.SemaphoreType.DMA((n_cond // 2, n_val)),
         ],
         compiler_params=pltpu.CompilerParams(
             vmem_limit_bytes=62 * 2**20, collective_id=0, has_side_effects=True
@@ -398,16 +430,19 @@
     )(flat_rows(orb_val), flat_rows(orb_cond), gvec_map.reshape(1, count_g), energies, *matrices)
     high = n_cond * n_val * 16
     return pl.pallas_call(
-        functools.partial(chi_kernel, row_segs, col_segs),
+        functools.partial(chi_kernel, col_segs),
         grid=(row_segs,),
         out_shape=jax.ShapeDtypeStruct((2, row_block, col_block), F32),
-        in_specs=[vmem, vmem],
+        in_specs=[hbm, hbm],
         out_specs=pl.BlockSpec((2, row_lanes, col_block), lambda seg: (0, seg, 0)),
         scratch_shapes=[
+            pltpu.VMEM((high, row_lanes), BF16),
+            pltpu.VMEM((high, col_lanes), BF16),
             pltpu.VMEM((row_lanes // 128, high, 128), F32),
             pltpu.VMEM((high // 8, 2 * col_block), BF16),
+            pltpu.SemaphoreType.DMA((2,)),
         ],
-        compiler_params=pltpu.CompilerParams(vmem_limit_bytes=48 * 2**20),
+        compiler_params=pltpu.CompilerParams(vmem_limit_bytes=62 * 2**20),
         name="chi",
     )(rows_all.reshape(high, row_lanes), cols_all.reshape(high, col_lanes))
 

time: 30.9 us -> 34.9 us (1.13)
  Pallas kernels: 28.9 us -> 34.7 us
  local copies, waits for them, and re-layouts: 1.85 us -> 0 us
    pallas_call x1, Pallas kernels: 20.8 us -> 25.7 us  [on_device(): pl.pallas_call(functools.partial(density_kernel, reach, counts), out_shap...]
    unnamed x4 -> x0, local copies, waits for them, and re-layouts: 1.85 us -> none
    pallas_call x1, Pallas kernels: 8.06 us -> 8.98 us  [on_device(): pl.pallas_call(functools.partial(chi_kernel, col_segs), grid=(row_segs,),...]
where the time goes in v4:
time: 34.9 us; the launch traced here: 34.7 us
  Pallas kernels  34.7 us (99%)
    pallas_call x1, Pallas kernels, on_device(): pl.pallas_call(functools.partial(density_kernel, reach, counts), out_shap...  25.7 us
    pallas_call x1, Pallas kernels, on_device(): pl.pallas_call(functools.partial(chi_kernel, col_segs), grid=(row_segs,),...  8.98 us

profile of v4, /device:TPU:0, one launch (start us, length us, event | category | flops | bytes accessed | tf_op | source)
XLA Modules:
  0.0 34.7 jit_solution(7520435488111499497)
XLA Ops:
  0.0 25.7 %density.1 = (bf16[8,4,16,256]{3,2,1,0:T(8,128)(2,1)}, bf16[8,4,16,128]{3,2,1,0:T(8,128)(2,1)}) custom-call(bf16[4096,128]{1,0:T(8,128)(2,1)} %bitcast.13, bf16[4096,128]{1,0:T(8,128)(2,1)} %bitcast.14, s32[1,8192]{1,0:T(1,128)} %bitcast.17, f32[4,8]{1,0:T(4,128)} %energy_in.1, bf16[768,128]{1,0:T(8,128)(2,1)} %constant.6.clone.wz_ref, ...), custom_call_target="tpu_custom_call" | custom-call | tf_op jit(solution)/shard_map/density/pallas_call | solution.py:396
  25.7 9.0 %chi.1 = f32[2,2048,1024]{2,1,0:T(8,128)} custom-call(bf16[512,256]{1,0:T(8,128)(2,1)} %bitcast.15, bf16[512,128]{1,0:T(8,128)(2,1)} %bitcast.16), custom_call_target="tpu_custom_call" | custom-call | tf_op jit(solution)/shard_map/chi/pallas_call | solution.py:432
